TPU v7x, 512 devices: a whole 4x4x16 slice. The times are simulated.
512 devices in a mesh: dp: 64 (over x, z), sub: 8 (over y, core).
Axes of the slice: x: 4, y: 4, z: 16, core: 2. Of those that a mesh axis runs over, the one named last changes fastest.
Arguments:
- points: bfloat16 [65536, 768], P(('dp', 'sub'))
- cand_rows: int32 [3, 2048], P(None, ('dp', 'sub')), may hold values from 0 to 127
- cand_count: int32 [3, 512], P(None, ('dp', 'sub')), may hold values from 0 to 4, as said below
Outputs:
- weights: float32 [3, 65536], P(None, ('dp', 'sub'))
Inputs may be any that keep to these rules, and one draw needn't show every extreme that they name: `cand_rows`: local row numbers on the device whose slots they fill; slots at or past the count are ignored. `cand_count`: in every round the devices of each group along sub hold exactly 16 candidates together; in every round some device holds 4.
All inputs are finite; a program needn't handle non-finite values.
Results may differ from a plain program's by a relative error of at most 0.0003.
Values may be sent and summed in bfloat16 or wider, within the bound.
A program may use at most 64 MiB of HBM per device.

v0:
```python
import jax
import jax.numpy as jnp
from jax import lax
from jax.experimental import pallas as pl
from jax.experimental.pallas import tpu as pltpu
from jax.sharding import PartitionSpec as P

ROUNDS = 3
SLOTS = 4
XS = 4
ZS = 16
YS = 4
SUBS = 8
RAW = 16
BLK = 8
SHARE = 2
USED_ROWS = pl.ds(0, ROUNDS * SHARE)
NEAR = 9
MESH = pl.DeviceIdType.MESH
F32 = jnp.float32
INF = float("inf")


def kernel(
    npts,
    rows_in,
    counts_in,
    points_ref,
    out_ref,
    rows_ref,
    cnt_ref,
    raw,
    slots,
    cand,
    pall,
    mins,
    squares,
    line,
    near,
    zsum,
    ysum,
    local_sem,
    slots_send,
    slots_recv,
    z_block_send,
    y_send,
    z_block_recv,
    y_recv,
    far_send,
    far_z_send,
    far_recv,
    far_z_recv,
    pts_send,
    pts_recv,
    line_send,
    line_recv,
    z_send,
    z_recv,
    c_send,
    c_recv,
):
    dp = lax.axis_index("dp")
    sub = lax.axis_index("sub")
    x, z = lax.div(dp, ZS), lax.rem(dp, ZS)
    y, core = lax.div(sub, 2), lax.rem(sub, 2)
    npd, width = points_ref.shape

    def at_x(d):
        return (lax.rem(x + d, XS) * ZS + z, sub)

    def at_z(d):
        return (x * ZS + lax.rem(z + d, ZS), sub)

    def at_y(d):
        return (dp, lax.rem(y + d, YS) * 2 + core)

    other_core = (dp, y * 2 + (1 - core))
    z_to = {d: at_z(d % ZS) for d in (1, -1, 2, -2, 3, -3, 4, -4)}
    y_to = {d: at_y(d) for d in (1, 2, 3)}
    me = x * 2 + core
    x_right, x_left = at_x(1), at_x(3)

    own_points = pltpu.make_async_copy(points_ref, raw, local_sem.at[0])
    own_points.start()
    own_rows = pltpu.make_async_copy(rows_in, rows_ref, local_sem.at[1])
    own_rows.start()
    own_counts = pltpu.make_async_copy(counts_in, cnt_ref, local_sem.at[2])
    own_counts.start()
    barrier = pltpu.get_barrier_semaphore()
    far_first = ((2, 0), (2, 1), (1, 0), (3, 0), (1, 1), (3, 1), (0, 1))
    y_line = [(dp, lax.rem(y + d, YS) * 2 + (1 - core if other else core)) for d, other in far_first]
    x_line = [(lax.rem(x + d, XS) * ZS + z, y * 2 + (1 - core if other else core)) for d, other in far_first]
    partners = [*z_to.values(), *y_line, *x_line[:-1]]
    for device in partners:
        pl.semaphore_signal(barrier, inc=1, device_id=device, device_id_type=MESH)

    row = lax.broadcasted_iota(jnp.int32, (RAW, npd), 0)
    lane = lax.broadcasted_iota(jnp.int32, (RAW, npd), 1)
    here = lax.broadcasted_iota(jnp.int32, (npd, npd), 0)
    there = lax.broadcasted_iota(jnp.int32, (npd, npd), 1)
    same_round = (here & (RAW - 1)) == ROUNDS * SLOTS + ((there & (RAW - 1)) >> 2)
    before = jnp.where(same_round & ((here >> 4) < (there >> 4)), 1.0, 0.0)
    itself = jnp.where(same_round & ((here >> 4) == (there >> 4)), 1.0, 0.0)
    slot = lane & (RAW - 1)
    slot_round = jnp.where(slot < ROUNDS * SLOTS, slot >> 2, -1)
    slot_index = (slot & (SLOTS - 1)).astype(F32)
    wanted = (SHARE * sub + (row & 1)).astype(F32)
    wanted_round = slot_round == (row >> 1)
    own_rows.wait()
    own_counts.wait()
    target = jnp.full((RAW, npd), -1, jnp.int32)
    counts = jnp.zeros((RAW, npd), F32)
    for r in range(ROUNDS):
        counts = jnp.where(row == ROUNDS * SLOTS + r, cnt_ref[0, r].astype(F32), counts)
        for i in range(SLOTS):
            target = jnp.where(row == r * SLOTS + i, rows_ref[r, i], target)
    pick = jnp.where(lane == target, 1.0, 0.0).astype(jnp.bfloat16)
    own_points.wait()
    mine = raw[...]
    block = jnp.dot(pick, mine, preferred_element_type=F32)
    slots[sub, :, :npd] = (block[:, :npd] + counts).astype(jnp.bfloat16)
    slots[sub, :, npd:] = block[:, npd:].astype(jnp.bfloat16)

    pl.semaphore_wait(barrier, len(partners))

    def remote(src, dst, send, recv, device):
        return pltpu.make_async_remote_copy(
            src_ref=src, dst_ref=dst, send_sem=send, recv_sem=recv, device_id=device, device_id_type=MESH
        )

    def to_sides(place, count, group):
        for d, column in ((1, 2), (3, 3)):
            src, dst = cand.at[0, pl.ds(place, count), USED_ROWS], cand.at[column, pl.ds(place, count), USED_ROWS]
            remote(src, dst, y_send, y_recv.at[group], y_to[d]).start()

    def to_far(place):
        remote(cand.at[0, place, USED_ROWS], cand.at[1, place, USED_ROWS], far_send, far_recv.at[place - 6], y_to[2]).start()

    def far_along_z(src, place, count, group, d, lanes=None):
        src, dst = cand.at[1, pl.ds(src, count), USED_ROWS], cand.at[1, pl.ds(place, count), USED_ROWS]
        if lanes is not None:
            part = pl.ds(lanes * (width // 2), width // 2)
            src, dst = src.at[:, :, part], dst.at[:, :, part]
        remote(src, dst, far_z_send, far_z_recv.at[group], z_to[d]).start()

    def along_z(src, place, d, lanes=None):
        if lanes is None:
            src, dst = cand.at[0, src, USED_ROWS], cand.at[0, place, USED_ROWS]
        else:
            part = pl.ds(lanes * (width // 2), width // 2)
            src, dst = cand.at[0, src, USED_ROWS, part], cand.at[0, place, USED_ROWS, part]
        remote(src, dst, z_block_send, z_block_recv.at[place + (lanes or 0)], z_to[d]).start()

    def z_arrived(*places):
        for place in places:
            wait_bytes(cand.at[0, place, USED_ROWS], z_block_recv.at[place])

    def wait_bytes(ref, sem):
        pltpu.make_async_copy(ref, ref, sem).wait()

    for device in y_line:
        remote(slots.at[sub], slots.at[sub], slots_send, slots_recv, device).start()
    pall[me] = mine.T
    slot_right, slot_left, slot_far = (lax.rem(x + d, XS) * 2 + core for d in (1, 3, 2))
    top, low = pl.ds(0, width // 2), pl.ds(width // 2, width // 2)
    mine_at = pall.at[me]
    pts_right = remote(mine_at, mine_at, pts_send.at[0], pts_recv.at[0], x_right)
    pts_left = remote(mine_at, mine_at, pts_send.at[1], pts_recv.at[1], x_left)
    pts_core = remote(mine_at, mine_at, pts_send.at[2], pts_recv.at[2], other_core)
    pts_right.start()
    pts_left.start()
    pts_core.start()

    wait_bytes(slots.at[pl.ds(0, SUBS - 1)], slots_recv)
    flat = slots[...].reshape(SUBS * RAW, width)
    known = flat[:, :npd].astype(F32)
    offset = jnp.sum(known * before, axis=0, keepdims=True)
    count = jnp.sum(known * itself, axis=0, keepdims=True)
    choice = wanted_round & (slot_index < count) & (offset + slot_index == wanted)
    share = jnp.dot(jnp.where(choice, 1.0, 0.0).astype(jnp.bfloat16), flat, preferred_element_type=F32)
    cand[0, 7] = share[:BLK].astype(jnp.bfloat16)

    along_z(7, 6, 4)
    along_z(7, 8, -4)
    to_far(7)
    for place, d in ((0, 2), (1, -2), (2, 1), (5, -1)):
        along_z(7, place, d)
    to_sides(7, 1, 0)

    pts_right.wait_recv()
    near_left = pall.at[slot_left]
    far_top = remote(near_left.at[top], near_left.at[top], pts_send.at[3], pts_recv.at[3], x_right)
    core_left = remote(near_left, near_left, pts_send.at[4], pts_recv.at[4], other_core)
    far_top.start()
    core_left.start()
    pts_left.wait_recv()
    near_right = pall.at[slot_right]
    far_low = remote(near_right.at[low], near_right.at[low], pts_send.at[5], pts_recv.at[5], x_left)
    core_right = remote(near_right, near_right, pts_send.at[6], pts_recv.at[6], other_core)
    far_low.start()
    core_right.start()

    z_arrived(6)
    to_far(6)
    along_z(6, 15, 4, 0)
    for place, d in ((13, 3), (9, 2), (11, 1), (4, -1)):
        along_z(6, place, d)
    z_arrived(8)
    to_far(8)
    along_z(8, 15, -4, 1)
    for place, d in ((14, -3), (10, -2), (12, -1), (3, 1)):
        along_z(8, place, d)
    to_sides(6, 1, 0)
    to_sides(8, 1, 0)

    for place in (6, 7, 8):
        wait_bytes(cand.at[1, place, USED_ROWS], far_recv.at[place - 6])
    far_along_z(6, 15, 1, 1, 4, 0)
    far_along_z(8, 15, 1, 1, -4, 1)
    far_along_z(6, 13, 1, 1, 3)
    far_along_z(8, 14, 1, 1, -3)
    far_along_z(6, 9, 1, 1, 2)
    far_along_z(8, 10, 1, 1, -2)
    far_along_z(6, 11, 1, 1, 1)
    far_along_z(8, 12, 1, 1, -1)
    far_along_z(7, 0, 1, 0, 2)
    far_along_z(7, 1, 1, 0, -2)
    far_along_z(7, 2, 2, 0, 1)
    far_along_z(6, 4, 2, 0, -1)

    far_top.wait_recv()
    far_low.wait_recv()
    far = pall.at[slot_far]
    core_far = remote(far, far, pts_send.at[7], pts_recv.at[7], other_core)
    core_far.start()

    z_arrived(0, 1, 2, 3, 4, 5)
    to_sides(0, 6, 0)
    z_arrived(9, 10, 11, 12, 13, 14)
    to_sides(9, 6, 1)
    half_block = cand.at[0, 15, USED_ROWS, pl.ds(0, width // 2)]
    wait_bytes(half_block, z_block_recv.at[15])
    wait_bytes(half_block, z_block_recv.at[16])
    to_sides(15, 1, 1)

    def absorb(first, count):
        blocks = XS * count
        rows = cand[:, first : first + count].reshape(blocks, BLK, width)
        half = jnp.zeros((blocks, BLK, npd), F32)
        for t in range(width // npd):
            piece = rows[:, :, t * npd : (t + 1) * npd].astype(F32)
            half = half + piece * piece
        half = 0.5 * jnp.sum(half, axis=2, keepdims=True)
        flat = rows.reshape(blocks * BLK, width)
        for j in range(SUBS // 2):
            group = jnp.concatenate([pall[2 * j], pall[2 * j + 1]], axis=1)
            dots = jnp.dot(flat, group, preferred_element_type=F32)
            best = jnp.min(half - dots.reshape(blocks, BLK, 2 * npd), axis=0)
            mins[j] = best if first == 0 else jnp.minimum(mins[j], best)

    pts_core.wait_recv()
    core_left.wait_recv()
    core_right.wait_recv()
    core_far.wait_recv()
    for b in range(SUBS):
        wide = pall[b].astype(F32)
        squares[b : b + 1, :] = jnp.sum(wide * wide, axis=0, keepdims=True)
    wait_bytes(cand.at[pl.ds(2, 2), pl.ds(0, NEAR), USED_ROWS], y_recv.at[0])
    wait_bytes(cand.at[1, pl.ds(0, 6), USED_ROWS], far_z_recv.at[0])
    absorb(0, NEAR)
    wait_bytes(cand.at[pl.ds(2, 2), pl.ds(NEAR, ZS - NEAR), USED_ROWS], y_recv.at[1])
    wait_bytes(cand.at[1, pl.ds(NEAR, ZS - NEAR), USED_ROWS], far_z_recv.at[1])
    absorb(NEAR, ZS - NEAR)

    for j in range(SUBS // 2):
        for r in range(ROUNDS):
            low_r = jnp.min(mins[j, r * SHARE : (r + 1) * SHARE, :], axis=0, keepdims=True)
            for h in range(2):
                line[me, r, 2 * j + h : 2 * j + h + 1, :] = low_r[:, h * npd : (h + 1) * npd]

    for device in x_line:
        remote(line.at[me], line.at[me], line_send, line_recv, device).start()
    wait_bytes(line.at[pl.ds(0, SUBS - 1)], line_recv)

    lanes = lax.broadcasted_iota(jnp.int32, (1, npd), 1)
    least = None
    total = jnp.zeros((1, npd), F32)
    for r in range(ROUNDS):
        now = jnp.min(line[:, r], axis=0)
        least = now if least is None else jnp.minimum(least, now)
        dist = jnp.maximum(squares[...] + 2.0 * least, 0.0)
        near[r] = dist
        part = jnp.sum(jnp.sum(dist, axis=0, keepdims=True), axis=1, keepdims=True)
        total = jnp.where(lanes == r, part, total)

    zsum[0] = total

    for d in (8, 7, 9, 6, 10, 5, 11, 4, 12, 3, 13, 2, 14, 1, 15):
        remote(zsum.at[0], zsum.at[ZS - d], z_send, z_recv, at_z(d)).start()
    wait_bytes(slots.at[pl.ds(0, SUBS - 1)], slots_send)
    wait_bytes(cand.at[0, pl.ds(0, 15), USED_ROWS], z_block_send)
    wait_bytes(cand.at[pl.ds(0, 2), :, USED_ROWS], y_send)
    wait_bytes(cand.at[0, pl.ds(0, 3), USED_ROWS], far_send)
    wait_bytes(cand.at[0, pl.ds(0, 13), USED_ROWS], far_z_send)
    for copy in (pts_right, pts_left, pts_core, far_top, core_left, far_low, core_right, core_far):
        copy.wait_send()
    wait_bytes(line.at[pl.ds(0, SUBS - 1)], line_send)
    wait_bytes(zsum.at[pl.ds(0, ZS - 1)], z_recv)
    ysum[0] = jnp.sum(zsum[...], axis=0)
    for d in (1, 3, 2):
        remote(ysum.at[0], ysum.at[XS - d], c_send, c_recv, y_to[d]).start()
    wait_bytes(ysum.at[pl.ds(0, XS - 1)], c_recv)
    cost = jnp.sum(ysum[...], axis=0)
    for r in range(ROUNDS):
        cost_r = jnp.sum(jnp.where(lanes == r, cost, 0.0), axis=1, keepdims=True)
        out_ref[r : r + 1, :] = npts * near[r, pl.ds(me, 1), :] / cost_r
    wait_bytes(zsum.at[pl.ds(0, ZS - 1)], z_send)
    wait_bytes(ysum.at[pl.ds(0, XS - 1)], c_send)


def shards(points, cand_rows, cand_count):
    npd, width = points.shape
    npts = float(npd * lax.axis_size(("dp", "sub")))
    dma = pltpu.SemaphoreType.DMA
    operands = (cand_rows, cand_count.reshape(1, ROUNDS), points)
    return pl.pallas_call(
        lambda *refs: kernel(npts, *refs),
        out_shape=jax.ShapeDtypeStruct((ROUNDS, npd), F32),
        in_specs=[
            pl.BlockSpec(memory_space=pl.ANY),
            pl.BlockSpec(memory_space=pl.ANY),
            pl.BlockSpec(memory_space=pl.ANY),
        ],
        out_specs=pl.BlockSpec(memory_space=pltpu.VMEM),
        scratch_shapes=[
            pltpu.SMEM((ROUNDS, SLOTS), jnp.int32),
            pltpu.SMEM((1, ROUNDS), jnp.int32),
            pltpu.VMEM((npd, width), jnp.bfloat16),
            pltpu.VMEM((SUBS, RAW, width), jnp.bfloat16),
            pltpu.VMEM((XS, ZS, BLK, width), jnp.bfloat16),
            pltpu.VMEM((SUBS, width, npd), jnp.bfloat16),
            pltpu.VMEM((SUBS // 2, BLK, 2 * npd), F32),
            pltpu.VMEM((SUBS, npd), F32),
            pltpu.VMEM((SUBS, ROUNDS, SUBS, npd), F32),
            pltpu.VMEM((ROUNDS, SUBS, npd), F32),
            pltpu.VMEM((ZS, 1, npd), F32),
            pltpu.VMEM((XS, 1, npd), F32),
            dma((3,)),
            dma,
            dma,
            dma,
            dma,
            dma((17,)),
            dma((2,)),
            dma,
            dma,
            dma((3,)),
            dma((2,)),
            dma((8,)),
            dma((8,)),
            dma,
            dma,
            dma,
            dma,
            dma,
            dma,
        ],
        compiler_params=pltpu.CompilerParams(
            collective_id=0, has_side_effects=True, vmem_limit_bytes=40 * 1024 * 1024
        ),
        cost_estimate=pl.CostEstimate(
            flops=2 * 1024 * 1024 * width, bytes_accessed=npd * width * 2, transcendentals=0
        ),
    )(*(pltpu.with_memory_space_constraint(value, pltpu.HBM) for value in operands))


def solution(mesh):
    in_specs = (P(("dp", "sub"), None), P(None, ("dp", "sub")), P(None, ("dp", "sub")))
    out_specs = P(None, ("dp", "sub"))
    return jax.shard_map(shards, mesh=mesh, in_specs=in_specs, out_specs=out_specs, check_vma=False)
```

profile of v0, /device:TPU:1, one launch (start us, length us, event | category | flops | bytes accessed | tf_op | source)
XLA Modules:
  0.0 46.4 jit_solution(11902192591269599625)
XLA Ops:
  0.0 45.8 %shard_map.37 = f32[3,128]{1,0:T(4,128)S(1)} custom-call(s32[3,4]{1,0:T(4,128)} %refs_0_.1, s32[1,3]{1,0:T(1,128)} %bitcast.1, bf16[128,768]{1,0:T(8,128)(2,1)} %refs_2_.1), custom_call_target="tpu_custom_call" | custom-call | flops 1610612736 | bytes 196608 | tf_op jit(solution)/shard_map/pallas_call | solution.py:326
  45.8 0.6 %copy.5 = f32[3,128]{1,0:T(4,128)} copy(f32[3,128]{1,0:T(4,128)S(1)} %shard_map.37) | data formatting | bytes 3072
where the time goes:
time: 46.5 us; the launch traced here: 46.4 us
  Pallas kernels  45.8 us (98%)
  local copies, waits for them, and re-layouts  0.58 us (1%)
    pallas_call x1, Pallas kernels, shards(): pl.pallas_call(lambda *refs: kernel(npts, *refs), out_shape=jax.ShapeDtyp...  45.8 us

commit v1 on v0

--- a/solution.py
+++ b/solution.py
@@ -90,7 +90,7 @@
     far_first = ((2, 0), (2, 1), (1, 0), (3, 0), (1, 1), (3, 1), (0, 1))
     y_line = [(dp, lax.rem(y + d, YS) * 2 + (1 - core if other else core)) for d, other in far_first]
     x_line = [(lax.rem(x + d, XS) * ZS + z, y * 2 + (1 - core if other else core)) for d, other in far_first]
-    partners = [*z_to.values(), *y_line, *x_line[:-1]]
+    partners = [*(z_to[d] for d in (4, -4, 2, -2, 1, -1)), *y_line, x_right, x_left]
     for device in partners:
         pl.semaphore_signal(barrier, inc=1, device_id=device, device_id_type=MESH)
 
@@ -203,12 +203,14 @@
     z_arrived(6)
     to_far(6)
     along_z(6, 15, 4, 0)
-    for place, d in ((13, 3), (9, 2), (11, 1), (4, -1)):
+    for place, d in ((9, 2), (11, 1), (4, -1)):
         along_z(6, place, d)
     z_arrived(8)
     to_far(8)
     along_z(8, 15, -4, 1)
-    for place, d in ((14, -3), (10, -2), (12, -1), (3, 1)):
+    along_z(8, 14, -3)
+    along_z(6, 13, 3)
+    for place, d in ((10, -2), (12, -1), (3, 1)):
         along_z(8, place, d)
     to_sides(6, 1, 0)
     to_sides(8, 1, 0)

time: 46.5 us -> 46.4 us (level)
  no operation moved by 1% of the time
where the time goes in v1:
time: 46.4 us; the launch traced here: 46.3 us
  Pallas kernels  45.7 us (98%)
  local copies, waits for them, and re-layouts  0.58 us (1%)
    pallas_call x1, Pallas kernels, shards(): pl.pallas_call(lambda *refs: kernel(npts, *refs), out_shape=jax.ShapeDtyp...  45.7 us

profile of v1, /device:TPU:1, one launch (start us, length us, event | category | flops | bytes accessed | tf_op | source)
XLA Modules:
  0.0 46.3 jit_solution(7692685204695393137)
XLA Ops:
  0.0 45.7 %shard_map.37 = f32[3,128]{1,0:T(4,128)S(1)} custom-call(s32[3,4]{1,0:T(4,128)} %refs_0_.1, s32[1,3]{1,0:T(1,128)} %bitcast.1, bf16[128,768]{1,0:T(8,128)(2,1)} %refs_2_.1), custom_call_target="tpu_custom_call" | custom-call | flops 1610612736 | bytes 196608 | tf_op jit(solution)/shard_map/pallas_call | solution.py:328
  45.7 0.6 %copy.5 = f32[3,128]{1,0:T(4,128)} copy(f32[3,128]{1,0:T(4,128)S(1)} %shard_map.37) | data formatting | bytes 3072

commit v2 on v0

--- a/solution.py
+++ b/solution.py
@@ -16,6 +16,7 @@
 SHARE = 2
 USED_ROWS = pl.ds(0, ROUNDS * SHARE)
 NEAR = 9
+HALF = ZS // 2
 MESH = pl.DeviceIdType.MESH
 F32 = jnp.float32
 INF = float("inf")
@@ -37,6 +38,7 @@
     squares,
     line,
     near,
+    line_sum,
     zsum,
     ysum,
     local_sem,
@@ -293,10 +295,29 @@
         part = jnp.sum(jnp.sum(dist, axis=0, keepdims=True), axis=1, keepdims=True)
         total = jnp.where(lanes == r, part, total)
 
-    zsum[0] = total
-
-    for d in (8, 7, 9, 6, 10, 5, 11, 4, 12, 3, 13, 2, 14, 1, 15):
-        remote(zsum.at[0], zsum.at[ZS - d], z_send, z_recv, at_z(d)).start()
+    line_sum[...] = total
+
+    @pl.when(core == 0)
+    def _():
+        zsum[0] = total
+
+    @pl.when(core == 1)
+    def _():
+        remote(line_sum, zsum.at[0], z_send, z_recv, at_z(HALF)).start()
+
+    for k in range(HALF - 1):
+        place = HALF - 1 - k + core * (2 * k + 2 - HALF)
+        remote(line_sum, zsum.at[place], z_send, z_recv, at_z(HALF * core + place)).start()
+
+    def wait_z(sem):
+        @pl.when(core == 0)
+        def _():
+            wait_bytes(zsum.at[pl.ds(0, HALF - 1)], sem)
+
+        @pl.when(core == 1)
+        def _():
+            wait_bytes(zsum, sem)
+
     wait_bytes(slots.at[pl.ds(0, SUBS - 1)], slots_send)
     wait_bytes(cand.at[0, pl.ds(0, 15), USED_ROWS], z_block_send)
     wait_bytes(cand.at[pl.ds(0, 2), :, USED_ROWS], y_send)
@@ -305,17 +326,17 @@
     for copy in (pts_right, pts_left, pts_core, far_top, core_left, far_low, core_right, core_far):
         copy.wait_send()
     wait_bytes(line.at[pl.ds(0, SUBS - 1)], line_send)
-    wait_bytes(zsum.at[pl.ds(0, ZS - 1)], z_recv)
+    wait_z(z_recv)
     ysum[0] = jnp.sum(zsum[...], axis=0)
-    for d in (1, 3, 2):
-        remote(ysum.at[0], ysum.at[XS - d], c_send, c_recv, y_to[d]).start()
-    wait_bytes(ysum.at[pl.ds(0, XS - 1)], c_recv)
+    for (d, other), device in zip(far_first, y_line):
+        remote(ysum.at[0], ysum.at[(YS - d) % YS * 2 + other], c_send, c_recv, device).start()
+    wait_bytes(ysum.at[pl.ds(0, SUBS - 1)], c_recv)
     cost = jnp.sum(ysum[...], axis=0)
     for r in range(ROUNDS):
         cost_r = jnp.sum(jnp.where(lanes == r, cost, 0.0), axis=1, keepdims=True)
         out_ref[r : r + 1, :] = npts * near[r, pl.ds(me, 1), :] / cost_r
-    wait_bytes(zsum.at[pl.ds(0, ZS - 1)], z_send)
-    wait_bytes(ysum.at[pl.ds(0, XS - 1)], c_send)
+    wait_z(z_send)
+    wait_bytes(ysum.at[pl.ds(0, SUBS - 1)], c_send)
 
 
 def shards(points, cand_rows, cand_count):
@@ -343,8 +364,9 @@
             pltpu.VMEM((SUBS, npd), F32),
             pltpu.VMEM((SUBS, ROUNDS, SUBS, npd), F32),
             pltpu.VMEM((ROUNDS, SUBS, npd), F32),
-            pltpu.VMEM((ZS, 1, npd), F32),
-            pltpu.VMEM((XS, 1, npd), F32),
+            pltpu.VMEM((1, npd), F32),
+            pltpu.VMEM((HALF, 1, npd), F32),
+            pltpu.VMEM((SUBS, 1, npd), F32),
             dma((3,)),
             dma,
             dma,

time: 46.5 us -> 47.7 us (1.026)
  Pallas kernels: 45.8 us -> 47 us
    pallas_call x1, Pallas kernels: 45.8 us -> 47 us  [shards(): pl.pallas_call(lambda *refs: kernel(npts, *refs), out_shape=jax.ShapeDtyp...]
where the time goes in v2:
time: 47.7 us; the launch traced here: 47.6 us
  Pallas kernels  47 us (99%)
  local copies, waits for them, and re-layouts  0.58 us (1%)
    pallas_call x1, Pallas kernels, shards(): pl.pallas_call(lambda *refs: kernel(npts, *refs), out_shape=jax.ShapeDtyp...  47 us

profile of v2, /device:TPU:1, one launch (start us, length us, event | category | flops | bytes accessed | tf_op | source)
XLA Modules:
  0.0 47.6 jit_solution(11448068326043497746)
XLA Ops:
  0.0 47.0 %shard_map.37 = f32[3,128]{1,0:T(4,128)S(1)} custom-call(s32[3,4]{1,0:T(4,128)} %refs_0_.1, s32[1,3]{1,0:T(1,128)} %bitcast.1, bf16[128,768]{1,0:T(8,128)(2,1)} %refs_2_.1), custom_call_target="tpu_custom_call" | custom-call | flops 1610612736 | bytes 196608 | tf_op jit(solution)/shard_map/pallas_call | solution.py:347
  47.0 0.6 %copy.5 = f32[3,128]{1,0:T(4,128)} copy(f32[3,128]{1,0:T(4,128)S(1)} %shard_map.37) | data formatting | bytes 3072

commit v3 on v0

--- a/solution.py
+++ b/solution.py
@@ -236,8 +236,9 @@
 
     z_arrived(0, 1, 2, 3, 4, 5)
     to_sides(0, 6, 0)
-    z_arrived(9, 10, 11, 12, 13, 14)
-    to_sides(9, 6, 1)
+    for place in (11, 9, 13):
+        z_arrived(place, place + 1)
+        to_sides(place, 2, 1)
     half_block = cand.at[0, 15, USED_ROWS, pl.ds(0, width // 2)]
     wait_bytes(half_block, z_block_recv.at[15])
     wait_bytes(half_block, z_block_recv.at[16])

time: 46.5 us -> 46.5 us (level)
  no operation moved by 1% of the time
where the time goes in v3:
time: 46.5 us; the launch traced here: 46.4 us
  Pallas kernels  45.8 us (98%)
  local copies, waits for them, and re-layouts  0.58 us (1%)
    pallas_call x1, Pallas kernels, shards(): pl.pallas_call(lambda *refs: kernel(npts, *refs), out_shape=jax.ShapeDtyp...  45.8 us

profile of v3, /device:TPU:1, one launch (start us, length us, event | category | flops | bytes accessed | tf_op | source)
XLA Modules:
  0.0 46.4 jit_solution(9959504027649302433)
XLA Ops:
  0.0 45.8 %shard_map.37 = f32[3,128]{1,0:T(4,128)S(1)} custom-call(s32[3,4]{1,0:T(4,128)} %refs_0_.1, s32[1,3]{1,0:T(1,128)} %bitcast.1, bf16[128,768]{1,0:T(8,128)(2,1)} %refs_2_.1), custom_call_target="tpu_custom_call" | custom-call | flops 1610612736 | bytes 196608 | tf_op jit(solution)/shard_map/pallas_call | solution.py:327
  45.8 0.6 %copy.5 = f32[3,128]{1,0:T(4,128)} copy(f32[3,128]{1,0:T(4,128)S(1)} %shard_map.37) | data formatting | bytes 3072

commit v4 on v0

--- a/solution.py
+++ b/solution.py
@@ -35,6 +35,7 @@
     pall,
     mins,
     squares,
+    pair,
     line,
     near,
     zsum,
@@ -52,6 +53,8 @@
     far_z_recv,
     pts_send,
     pts_recv,
+    pair_send,
+    pair_recv,
     line_send,
     line_recv,
     z_send,
@@ -276,11 +279,15 @@
         for r in range(ROUNDS):
             low_r = jnp.min(mins[j, r * SHARE : (r + 1) * SHARE, :], axis=0, keepdims=True)
             for h in range(2):
-                line[me, r, 2 * j + h : 2 * j + h + 1, :] = low_r[:, h * npd : (h + 1) * npd]
-
-    for device in x_line:
-        remote(line.at[me], line.at[me], line_send, line_recv, device).start()
-    wait_bytes(line.at[pl.ds(0, SUBS - 1)], line_recv)
+                pair[0, r, 2 * j + h : 2 * j + h + 1, :] = low_r[:, h * npd : (h + 1) * npd]
+
+    swap = remote(pair.at[0], pair.at[1], pair_send, pair_recv, other_core)
+    swap.start()
+    swap.wait_recv()
+    line[0] = jnp.minimum(pair[0], pair[1])
+    for d in (2, 1, 3):
+        remote(line.at[0], line.at[XS - d], line_send, line_recv, at_x(d)).start()
+    wait_bytes(line.at[pl.ds(0, XS - 1)], line_recv)
 
     lanes = lax.broadcasted_iota(jnp.int32, (1, npd), 1)
     least = None
@@ -304,7 +311,8 @@
     wait_bytes(cand.at[0, pl.ds(0, 13), USED_ROWS], far_z_send)
     for copy in (pts_right, pts_left, pts_core, far_top, core_left, far_low, core_right, core_far):
         copy.wait_send()
-    wait_bytes(line.at[pl.ds(0, SUBS - 1)], line_send)
+    swap.wait_send()
+    wait_bytes(line.at[pl.ds(0, XS - 1)], line_send)
     wait_bytes(zsum.at[pl.ds(0, ZS - 1)], z_recv)
     ysum[0] = jnp.sum(zsum[...], axis=0)
     for d in (1, 3, 2):
@@ -341,7 +349,8 @@
             pltpu.VMEM((SUBS, width, npd), jnp.bfloat16),
             pltpu.VMEM((SUBS // 2, BLK, 2 * npd), F32),
             pltpu.VMEM((SUBS, npd), F32),
-            pltpu.VMEM((SUBS, ROUNDS, SUBS, npd), F32),
+            pltpu.VMEM((2, ROUNDS, SUBS, npd), F32),
+            pltpu.VMEM((XS, ROUNDS, SUBS, npd), F32),
             pltpu.VMEM((ROUNDS, SUBS, npd), F32),
             pltpu.VMEM((ZS, 1, npd), F32),
             pltpu.VMEM((XS, 1, npd), F32),
@@ -358,6 +367,8 @@
             dma((2,)),
             dma((8,)),
             dma((8,)),
+            dma,
+            dma,
             dma,
             dma,
             dma,

time: 46.5 us -> 46.7 us (level)
  no operation moved by 1% of the time
where the time goes in v4:
time: 46.7 us; the launch traced here: 46.6 us
  Pallas kernels  46 us (99%)
  local copies, waits for them, and re-layouts  0.58 us (1%)
    pallas_call x1, Pallas kernels, shards(): pl.pallas_call(lambda *refs: kernel(npts, *refs), out_shape=jax.ShapeDtyp...  46 us

profile of v4, /device:TPU:1, one launch (start us, length us, event | category | flops | bytes accessed | tf_op | source)
XLA Modules:
  0.0 46.6 jit_solution(6039768352720786058)
XLA Ops:
  0.0 46.0 %shard_map.37 = f32[3,128]{1,0:T(4,128)S(1)} custom-call(s32[3,4]{1,0:T(4,128)} %refs_0_.1, s32[1,3]{1,0:T(1,128)} %bitcast.1, bf16[128,768]{1,0:T(8,128)(2,1)} %refs_2_.1), custom_call_target="tpu_custom_call" | custom-call | flops 1610612736 | bytes 196608 | tf_op jit(solution)/shard_map/pallas_call | solution.py:334
  46.0 0.6 %copy.5 = f32[3,128]{1,0:T(4,128)} copy(f32[3,128]{1,0:T(4,128)S(1)} %shard_map.37) | data formatting | bytes 3072

commit v5 on v0

--- a/solution.py
+++ b/solution.py
@@ -104,8 +104,13 @@
     slot = lane & (RAW - 1)
     slot_round = jnp.where(slot < ROUNDS * SLOTS, slot >> 2, -1)
     slot_index = (slot & (SLOTS - 1)).astype(F32)
-    wanted = (SHARE * sub + (row & 1)).astype(F32)
-    wanted_round = slot_round == (row >> 1)
+    want = lax.broadcasted_iota(jnp.int32, (XS * BLK, npd), 0)
+    column = want >> 3
+    ahead = jnp.where(column == 1, 2, jnp.where(column == 2, 3, jnp.where(column == 3, 1, 0)))
+    holder = ((y + ahead) & (YS - 1)) * 2 + core
+    wanted = (SHARE * holder + (want & 1)).astype(F32)
+    wanted_round = slot_round[:1] == ((want & (BLK - 1)) >> 1)
+    slot_index = slot_index[:1]
     own_rows.wait()
     own_counts.wait()
     target = jnp.full((RAW, npd), -1, jnp.int32)
@@ -178,14 +183,12 @@
     count = jnp.sum(known * itself, axis=0, keepdims=True)
     choice = wanted_round & (slot_index < count) & (offset + slot_index == wanted)
     share = jnp.dot(jnp.where(choice, 1.0, 0.0).astype(jnp.bfloat16), flat, preferred_element_type=F32)
-    cand[0, 7] = share[:BLK].astype(jnp.bfloat16)
+    cand[:, 7] = share.reshape(XS, BLK, width).astype(jnp.bfloat16)
 
     along_z(7, 6, 4)
     along_z(7, 8, -4)
-    to_far(7)
     for place, d in ((0, 2), (1, -2), (2, 1), (5, -1)):
         along_z(7, place, d)
-    to_sides(7, 1, 0)
 
     pts_right.wait_recv()
     near_left = pall.at[slot_left]
@@ -213,7 +216,7 @@
     to_sides(6, 1, 0)
     to_sides(8, 1, 0)
 
-    for place in (6, 7, 8):
+    for place in (6, 8):
         wait_bytes(cand.at[1, place, USED_ROWS], far_recv.at[place - 6])
     far_along_z(6, 15, 1, 1, 4, 0)
     far_along_z(8, 15, 1, 1, -4, 1)
@@ -265,7 +268,7 @@
     for b in range(SUBS):
         wide = pall[b].astype(F32)
         squares[b : b + 1, :] = jnp.sum(wide * wide, axis=0, keepdims=True)
-    wait_bytes(cand.at[pl.ds(2, 2), pl.ds(0, NEAR), USED_ROWS], y_recv.at[0])
+    wait_bytes(cand.at[pl.ds(2, 2), pl.ds(0, NEAR - 1), USED_ROWS], y_recv.at[0])
     wait_bytes(cand.at[1, pl.ds(0, 6), USED_ROWS], far_z_recv.at[0])
     absorb(0, NEAR)
     wait_bytes(cand.at[pl.ds(2, 2), pl.ds(NEAR, ZS - NEAR), USED_ROWS], y_recv.at[1])
@@ -299,8 +302,8 @@
         remote(zsum.at[0], zsum.at[ZS - d], z_send, z_recv, at_z(d)).start()
     wait_bytes(slots.at[pl.ds(0, SUBS - 1)], slots_send)
     wait_bytes(cand.at[0, pl.ds(0, 15), USED_ROWS], z_block_send)
-    wait_bytes(cand.at[pl.ds(0, 2), :, USED_ROWS], y_send)
-    wait_bytes(cand.at[0, pl.ds(0, 3), USED_ROWS], far_send)
+    wait_bytes(cand.at[pl.ds(0, 2), pl.ds(0, 15), USED_ROWS], y_send)
+    wait_bytes(cand.at[0, pl.ds(0, 2), USED_ROWS], far_send)
     wait_bytes(cand.at[0, pl.ds(0, 13), USED_ROWS], far_z_send)
     for copy in (pts_right, pts_left, pts_core, far_top, core_left, far_low, core_right, core_far):
         copy.wait_send()

time: 46.5 us -> 46.5 us (level)
  no operation moved by 1% of the time
where the time goes in v5:
time: 46.5 us; the launch traced here: 46.4 us
  Pallas kernels  45.8 us (98%)
  local copies, waits for them, and re-layouts  0.58 us (1%)
    pallas_call x1, Pallas kernels, shards(): pl.pallas_call(lambda *refs: kernel(npts, *refs), out_shape=jax.ShapeDtyp...  45.8 us

profile of v5, /device:TPU:1, one launch (start us, length us, event | category | flops | bytes accessed | tf_op | source)
XLA Modules:
  0.0 46.4 jit_solution(15625690098035252251)
XLA Ops:
  0.0 45.8 %shard_map.37 = f32[3,128]{1,0:T(4,128)S(1)} custom-call(s32[3,4]{1,0:T(4,128)} %refs_0_.1, s32[1,3]{1,0:T(1,128)} %bitcast.1, bf16[128,768]{1,0:T(8,128)(2,1)} %refs_2_.1), custom_call_target="tpu_custom_call" | custom-call | flops 1610612736 | bytes 196608 | tf_op jit(solution)/shard_map/pallas_call | solution.py:329
  45.8 0.6 %copy.5 = f32[3,128]{1,0:T(4,128)} copy(f32[3,128]{1,0:T(4,128)S(1)} %shard_map.37) | data formatting | bytes 3072

commit v6 on v5

--- a/solution.py
+++ b/solution.py
@@ -213,8 +213,6 @@
     along_z(8, 15, -4, 1)
     for place, d in ((14, -3), (10, -2), (12, -1), (3, 1)):
         along_z(8, place, d)
-    to_sides(6, 1, 0)
-    to_sides(8, 1, 0)
 
     for place in (6, 8):
         wait_bytes(cand.at[1, place, USED_ROWS], far_recv.at[place - 6])
@@ -238,13 +236,12 @@
     core_far.start()
 
     z_arrived(0, 1, 2, 3, 4, 5)
-    to_sides(0, 6, 0)
+    to_sides(0, 7, 0)
     z_arrived(9, 10, 11, 12, 13, 14)
-    to_sides(9, 6, 1)
     half_block = cand.at[0, 15, USED_ROWS, pl.ds(0, width // 2)]
     wait_bytes(half_block, z_block_recv.at[15])
     wait_bytes(half_block, z_block_recv.at[16])
-    to_sides(15, 1, 1)
+    to_sides(8, 8, 1)
 
     def absorb(first, count):
         blocks = XS * count
@@ -268,12 +265,12 @@
     for b in range(SUBS):
         wide = pall[b].astype(F32)
         squares[b : b + 1, :] = jnp.sum(wide * wide, axis=0, keepdims=True)
-    wait_bytes(cand.at[pl.ds(2, 2), pl.ds(0, NEAR - 1), USED_ROWS], y_recv.at[0])
+    wait_bytes(cand.at[pl.ds(2, 2), pl.ds(0, 7), USED_ROWS], y_recv.at[0])
     wait_bytes(cand.at[1, pl.ds(0, 6), USED_ROWS], far_z_recv.at[0])
-    absorb(0, NEAR)
-    wait_bytes(cand.at[pl.ds(2, 2), pl.ds(NEAR, ZS - NEAR), USED_ROWS], y_recv.at[1])
+    absorb(0, 8)
+    wait_bytes(cand.at[pl.ds(2, 2), pl.ds(8, 8), USED_ROWS], y_recv.at[1])
     wait_bytes(cand.at[1, pl.ds(NEAR, ZS - NEAR), USED_ROWS], far_z_recv.at[1])
-    absorb(NEAR, ZS - NEAR)
+    absorb(8, 8)
 
     for j in range(SUBS // 2):
         for r in range(ROUNDS):

time: 46.5 us -> 46.6 us (level)
  no operation moved by 1% of the time
where the time goes in v6:
time: 46.6 us; the launch traced here: 46.5 us
  Pallas kernels  45.9 us (98%)
  local copies, waits for them, and re-layouts  0.58 us (1%)
    pallas_call x1, Pallas kernels, shards(): pl.pallas_call(lambda *refs: kernel(npts, *refs), out_shape=jax.ShapeDtyp...  45.9 us

profile of v6, /device:TPU:1, one launch (start us, length us, event | category | flops | bytes accessed | tf_op | source)
XLA Modules:
  0.0 46.5 jit_solution(16135004218420846351)
XLA Ops:
  0.0 45.9 %shard_map.37 = f32[3,128]{1,0:T(4,128)S(1)} custom-call(s32[3,4]{1,0:T(4,128)} %refs_0_.1, s32[1,3]{1,0:T(1,128)} %bitcast.1, bf16[128,768]{1,0:T(8,128)(2,1)} %refs_2_.1), custom_call_target="tpu_custom_call" | custom-call | flops 1610612736 | bytes 196608 | tf_op jit(solution)/shard_map/pallas_call | solution.py:326
  45.9 0.6 %copy.5 = f32[3,128]{1,0:T(4,128)} copy(f32[3,128]{1,0:T(4,128)S(1)} %shard_map.37) | data formatting | bytes 3072

commit v7 on v5

--- a/solution.py
+++ b/solution.py
@@ -15,7 +15,7 @@
 BLK = 8
 SHARE = 2
 USED_ROWS = pl.ds(0, ROUNDS * SHARE)
-NEAR = 9
+NEAR = 11
 MESH = pl.DeviceIdType.MESH
 F32 = jnp.float32
 INF = float("inf")
@@ -206,12 +206,12 @@
     z_arrived(6)
     to_far(6)
     along_z(6, 15, 4, 0)
-    for place, d in ((13, 3), (9, 2), (11, 1), (4, -1)):
+    for place, d in ((13, 3), (11, 2), (9, 1), (4, -1)):
         along_z(6, place, d)
     z_arrived(8)
     to_far(8)
     along_z(8, 15, -4, 1)
-    for place, d in ((14, -3), (10, -2), (12, -1), (3, 1)):
+    for place, d in ((14, -3), (12, -2), (10, -1), (3, 1)):
         along_z(8, place, d)
     to_sides(6, 1, 0)
     to_sides(8, 1, 0)
@@ -222,10 +222,10 @@
     far_along_z(8, 15, 1, 1, -4, 1)
     far_along_z(6, 13, 1, 1, 3)
     far_along_z(8, 14, 1, 1, -3)
-    far_along_z(6, 9, 1, 1, 2)
-    far_along_z(8, 10, 1, 1, -2)
-    far_along_z(6, 11, 1, 1, 1)
-    far_along_z(8, 12, 1, 1, -1)
+    far_along_z(6, 11, 1, 1, 2)
+    far_along_z(8, 12, 1, 1, -2)
+    far_along_z(6, 9, 1, 0, 1)
+    far_along_z(8, 10, 1, 0, -1)
     far_along_z(7, 0, 1, 0, 2)
     far_along_z(7, 1, 1, 0, -2)
     far_along_z(7, 2, 2, 0, 1)
@@ -239,8 +239,10 @@
 
     z_arrived(0, 1, 2, 3, 4, 5)
     to_sides(0, 6, 0)
-    z_arrived(9, 10, 11, 12, 13, 14)
-    to_sides(9, 6, 1)
+    z_arrived(9, 10)
+    to_sides(9, 2, 0)
+    z_arrived(11, 12, 13, 14)
+    to_sides(11, 4, 1)
     half_block = cand.at[0, 15, USED_ROWS, pl.ds(0, width // 2)]
     wait_bytes(half_block, z_block_recv.at[15])
     wait_bytes(half_block, z_block_recv.at[16])
@@ -269,7 +271,7 @@
         wide = pall[b].astype(F32)
         squares[b : b + 1, :] = jnp.sum(wide * wide, axis=0, keepdims=True)
     wait_bytes(cand.at[pl.ds(2, 2), pl.ds(0, NEAR - 1), USED_ROWS], y_recv.at[0])
-    wait_bytes(cand.at[1, pl.ds(0, 6), USED_ROWS], far_z_recv.at[0])
+    wait_bytes(cand.at[1, pl.ds(0, 8), USED_ROWS], far_z_recv.at[0])
     absorb(0, NEAR)
     wait_bytes(cand.at[pl.ds(2, 2), pl.ds(NEAR, ZS - NEAR), USED_ROWS], y_recv.at[1])
     wait_bytes(cand.at[1, pl.ds(NEAR, ZS - NEAR), USED_ROWS], far_z_recv.at[1])

time: 46.5 us -> 46.5 us (level)
  no operation moved by 1% of the time
where the time goes in v7:
time: 46.5 us; the launch traced here: 46.4 us
  Pallas kernels  45.8 us (98%)
  local copies, waits for them, and re-layouts  0.58 us (1%)
    pallas_call x1, Pallas kernels, shards(): pl.pallas_call(lambda *refs: kernel(npts, *refs), out_shape=jax.ShapeDtyp...  45.8 us

profile of v7, /device:TPU:1, one launch (start us, length us, event | category | flops | bytes accessed | tf_op | source)
XLA Modules:
  0.0 46.4 jit_solution(18389818707035711036)
XLA Ops:
  0.0 45.8 %shard_map.37 = f32[3,128]{1,0:T(4,128)S(1)} custom-call(s32[3,4]{1,0:T(4,128)} %refs_0_.1, s32[1,3]{1,0:T(1,128)} %bitcast.1, bf16[128,768]{1,0:T(8,128)(2,1)} %refs_2_.1), custom_call_target="tpu_custom_call" | custom-call | flops 1610612736 | bytes 196608 | tf_op jit(solution)/shard_map/pallas_call | solution.py:331
  45.8 0.6 %copy.5 = f32[3,128]{1,0:T(4,128)} copy(f32[3,128]{1,0:T(4,128)S(1)} %shard_map.37) | data formatting | bytes 3072
